TPU v7x, 32 devices: a whole 2x2x4 slice. The times are simulated.
32 devices in a mesh: dom: 2 (over y), row: 16 (over z, x, core).
Axes of the slice: x: 2, y: 2, z: 4, core: 2. Of those that a mesh axis runs over, the one named last changes fastest.
Arguments:
- memory: bfloat16 [65536, 256], P(('dom', 'row')), may hold values from -5 to 5
- node_time: int32 [65536], P(('dom', 'row')), may hold values from 0 to 999
- target: int32 [4, 16384], P(None, ('dom', 'row')), may hold values from -1 to 2047
- source: int32 [4, 16384], P(None, ('dom', 'row')), may hold values from 0 to 65535, as said below
- event_time: int32 [4, 16384], P(None, ('dom', 'row')), may hold values from 1000 to 2999
- edge_feat: bfloat16 [4, 16384, 128], P(None, ('dom', 'row')), may hold values from -5 to 5
- owner_group: int32 [4], replicated, may hold values from 0 to 1
- w_message: bfloat16 [768, 256], replicated, may hold values from -0.21875 to 0.21875
- frequency: float32 [128], replicated, may hold values from 0.001 to 0.1
- phase_shift: float32 [128], replicated, may hold values from -3.140625 to 3.140625
- w_input: bfloat16 [256, 768], replicated, may hold values from -0.375 to 0.375
- w_hidden: bfloat16 [256, 768], replicated, may hold values from -0.375 to 0.375
- bias_input: float32 [768], replicated, may hold values from -3 to 3
- bias_hidden: float32 [768], replicated, may hold values from -3 to 3
Outputs:
- new_memory: bfloat16 [65536, 256], P(('dom', 'row'))
Inputs may be any that keep to these rules, and one draw needn't show every extreme that they name: `target`: -1 marks a padded event row. `source`: values under 32768 name the event's own group, the rest the owner group of the batch; in each batch, of the events of one device at most 48 have a value v < 32768 with v // 2048 equal to one given r, and at most 16 have v >= 32768 with (v - 32768) // 2048 equal to one given r; on every device and batch some r reaches 48 and some r reaches 16.
All inputs are finite; a program needn't handle non-finite values.
Results may differ from a plain program's by a relative error of at most 0.0034.
Values may be sent and summed in bfloat16 or wider, within the bound.
A program may use at most 64 MiB of HBM per device.

v0:
```python
import functools

import jax
import jax.numpy as jnp
from jax import lax
from jax.experimental import pallas as pl
from jax.experimental.pallas import tpu as pltpu
from jax.sharding import PartitionSpec as P

MESH = pl.DeviceIdType.MESH
LANES = 128
BF = jnp.bfloat16
F32 = jnp.float32
I32 = jnp.int32


def iota(shape, dim):
    return lax.broadcasted_iota(I32, shape, dim)


def onehot(mask):
    return jnp.where(mask, 1.0, 0.0).astype(BF)


def dot(a, b):
    return jnp.dot(a, b, preferred_element_type=F32)


def kernel(
    cfg,
    mem_ref,
    nt_ref,
    tgt_ref,
    src_ref,
    et_ref,
    edge_ref,
    owner_ref,
    wm_ref,
    freq_ref,
    phase_ref,
    wi_ref,
    wh_ref,
    bi_ref,
    bh_ref,
    out_ref,
    ids_send,
    ids_recv,
    colid,
    gmat,
    send,
    recv,
    domr,
    fars,
    place,
    tmat,
    smat,
    touched,
    pmat,
    emat,
    cnt,
    mt,
    part,
    gh,
    msg,
    fresh,
    sems,
):
    doms, rows, nodes, events, width, batches, cap, ocap, ready = cfg
    me_d = lax.axis_index("dom")
    me_r = lax.axis_index("row")
    group_nodes = rows * nodes
    node_bits = nodes.bit_length() - 1
    own_rows = rows * cap
    far_rows = rows * ocap
    IDS_S, IDS_R, IDD_S, IDD_R = range(4)
    OWN_S, OWN_R, DOM_S, DOM_R, FAR_S, FAR_R = (4 + batches * i for i in range(6))

    def row_peer(k):
        return (me_d, lax.rem(me_r + k, rows))

    def dom_peer(q):
        return (lax.rem(me_d + q, doms), me_r)

    def push(src, dst, s, r, peer):
        pltpu.make_async_remote_copy(
            src_ref=src,
            dst_ref=dst,
            send_sem=sems.at[s],
            recv_sem=sems.at[r],
            device_id=peer,
            device_id_type=MESH,
        ).start()

    def drain(ref, s):
        pltpu.make_async_copy(ref, ref, sems.at[s]).wait()

    barrier = pltpu.get_barrier_semaphore()
    for k in range(1, rows):
        pl.semaphore_signal(barrier, inc=1, device_id=row_peer(k), device_id_type=MESH)
    for q in range(1, doms):
        pl.semaphore_signal(barrier, inc=1, device_id=dom_peer(q), device_id_type=MESH)

    stacked = jnp.concatenate(
        [tgt_ref[...], src_ref[...], et_ref[...], et_ref[...]], axis=0
    ).astype(F32)
    cols = stacked.T.astype(I32)
    lane_e = iota((events, events), 1)
    sub_e = iota((events, events), 0)
    lane = iota((events, LANES), 1)

    def locate(s):
        far = s >= group_nodes
        local = jnp.where(far, s - group_nodes, s)
        rel = jnp.bitwise_and((local >> node_bits) - me_r + rows, rows - 1)
        return far, local, rel, jnp.where(far, rel + rows, rel)

    acc_hi = jnp.zeros((rows * 8, LANES), F32)
    acc_lo = jnp.zeros((rows * 8, LANES), F32)
    a_row = iota((rows * 8, events), 0)
    for b in range(batches):
        far_c, _, rel_c, key_c = locate(cols[:, batches + b : batches + b + 1])
        _, local_r, rel_r, key_r = locate(src_ref[b : b + 1, :])
        ahead = jnp.logical_and(key_c == key_r, lane_e < sub_e)
        rank = jnp.sum(jnp.where(ahead, 1.0, 0.0), axis=1, keepdims=True).astype(I32)
        slot = jnp.where(far_c, rank + cap, rank)
        place[b] = jnp.where(far_c, own_rows + rel_c * ocap + rank, rel_c * cap + rank)
        marks = onehot(slot == lane)
        off = jnp.bitwise_and(local_r, nodes - 1) + 1
        mine = jnp.logical_and((a_row >> 3) == rel_r, jnp.bitwise_and(a_row, 7) == b)
        hi = jnp.where(mine, (off >> 8).astype(F32), 0.0).astype(BF)
        lo = jnp.where(mine, jnp.bitwise_and(off, 255).astype(F32), 0.0).astype(BF)
        acc_hi += dot(hi, marks)
        acc_lo += dot(lo, marks)
    ids_send[...] = (acc_hi * 256.0 + acc_lo).astype(I32) - 1
    ids_recv[0, 0:8, :] = ids_send[0:8, :]

    pl.semaphore_wait(barrier, rows - 1 + doms - 1)
    for k in range(1, rows):
        j = rows - k
        push(
            ids_send.at[pl.ds(k * 8, 8)],
            ids_recv.at[0, pl.ds(j * 8, 8)],
            IDS_S,
            IDS_R,
            row_peer(k),
        )
    drain(ids_recv.at[0, pl.ds(8, rows * 8 - 8)], IDS_R)
    for q in range(1, doms):
        push(ids_recv.at[0], ids_recv.at[doms - q], IDD_S, IDD_R, dom_peer(q))

    def spread(q):
        turned = ids_recv[q].astype(F32).T.astype(I32)
        for b in range(batches):
            for k in range(rows):
                col = turned[:, k * 8 + b : k * 8 + b + 1]
                if q == 0:
                    colid[b, k * cap : (k + 1) * cap, :] = jnp.broadcast_to(
                        col[:cap], (cap, LANES)
                    )
                at = own_rows + q * far_rows + k * ocap
                colid[b, at : at + ocap, :] = jnp.broadcast_to(
                    col[cap : cap + ocap], (ocap, LANES)
                )

    def build(b, start, count, to):
        step = LANES
        lanes = iota((step, LANES), 1)

        @pl.loop(0, count // step)
        def _(i):
            c = colid[b, pl.ds(pl.multiple_of(start + i * step, step), step), :]
            for j in range(nodes // LANES):
                gmat[
                    pl.ds(pl.multiple_of(to + i * step, step), step),
                    j * LANES : (j + 1) * LANES,
                ] = onehot(c == lanes + j * LANES)

    def gather(b, table, start, count):
        if ready:
            at = start
        else:
            at = 0
            build(b, start, count, 0)
        found = dot(gmat[at : at + count, :], table[...]).astype(BF)
        send[b, start : start + count, :] = found

    spread(0)
    if ready:
        build(0, 0, own_rows + far_rows, 0)
    if doms > 1:
        drain(ids_recv.at[pl.ds(1, doms - 1)], IDD_R)
    for q in range(1, doms):
        spread(q)
    if ready and doms > 1:
        build(0, own_rows + far_rows, (doms - 1) * far_rows, own_rows + far_rows)

    half = own_rows // 2
    for b in range(batches):
        table = mem_ref if b == 0 else out_ref
        for q in range(1, doms):
            at = own_rows + q * far_rows
            gather(b, table, at, far_rows)
            push(
                send.at[b, pl.ds(at, far_rows)],
                domr.at[b, doms - q - 1],
                DOM_S + b,
                DOM_R + b,
                dom_peer(q),
            )
        for h in range(2):
            gather(b, table, h * half, half)
            if h == 0:
                recv[b, 0:cap, :] = send[b, 0:cap, :]
            for k in range(max(1, h * rows // 2), (h + 1) * rows // 2):
                push(
                    send.at[b, pl.ds(k * cap, cap)],
                    recv.at[b, pl.ds((rows - k) * cap, cap)],
                    OWN_S + b,
                    OWN_R + b,
                    row_peer(k),
                )
        gather(b, table, own_rows, far_rows)

        t_col = cols[:, b : b + 1]
        t_row = tgt_ref[b : b + 1, :]
        t_wide = jnp.broadcast_to(t_col, (events, LANES))
        for j in range(nodes // LANES):
            tmat[:, j * LANES : (j + 1) * LANES] = onehot(t_wide == lane + j * LANES)
        mt[...] = dot(tmat[...], table[...]).astype(BF)

        owner = owner_ref[b : b + 1, :]
        if doms > 1:
            drain(domr.at[b], DOM_R + b)
        picked = send[b, own_rows : own_rows + far_rows, :].astype(F32)
        for q in range(1, doms):
            picked = jnp.where(
                owner == lax.rem(me_d + q, doms), domr[b, q - 1].astype(F32), picked
            )
        fars[b] = picked.astype(BF)
        for k in range(1, rows):
            push(
                fars.at[b, pl.ds(k * ocap, ocap)],
                recv.at[b, pl.ds(own_rows + (rows - k) * ocap, ocap)],
                FAR_S + b,
                FAR_R + b,
                row_peer(k),
            )
        recv[b, own_rows : own_rows + ocap, :] = fars[b, 0:ocap, :]

        same = jnp.logical_and(t_col == t_row, t_col >= 0)
        same_f = jnp.where(same, 1.0, 0.0)
        emat[...] = same_f.astype(BF)
        cnt[...] = jnp.maximum(jnp.sum(same_f, axis=1, keepdims=True), 1.0)
        before = jnp.sum(
            jnp.where(sub_e < lane_e, same_f, 0.0), axis=0, keepdims=True
        )
        s_row = jnp.where(before > 0.0, -1, t_row)

        @pl.loop(0, nodes // 256)
        def _(i):
            at = pl.multiple_of(i * 256, 256)
            hit = jnp.where(iota((256, events), 0) + at == s_row, 1.0, 0.0)
            smat[pl.ds(at, 256), :] = hit.astype(BF)
            touched[pl.ds(at, 256), :] = jnp.sum(hit, axis=1, keepdims=True)

        hi_part = dot(onehot((t_col >> 7) == iota((events, nodes // LANES), 1)), nt_ref[0])
        lo_part = dot(onehot((t_col >> 7) == iota((events, nodes // LANES), 1)), nt_ref[1])
        hit = jnp.bitwise_and(t_col, LANES - 1) == lane
        seen = jnp.sum(
            jnp.where(hit, hi_part * 256.0 + lo_part, 0.0), axis=1, keepdims=True
        )
        for p in range(b):
            times = jnp.where(
                t_col == tgt_ref[p : p + 1, :], et_ref[p : p + 1, :].astype(F32), 0.0
            )
            seen = jnp.maximum(seen, jnp.max(times, axis=1, keepdims=True))
        seen = jnp.where(t_col >= 0, seen, 0.0)
        elapsed = cols[:, 2 * batches + b : 2 * batches + b + 1].astype(F32) - seen
        encoded = jnp.cos(elapsed * freq_ref[...] + phase_ref[...]).astype(BF)
        tw = freq_ref.shape[1]
        part[...] = (
            dot(mt[...], wm_ref[:width, :])
            + dot(encoded, wm_ref[2 * width : 2 * width + tw, :])
            + dot(edge_ref[b], wm_ref[2 * width + tw :, :])
        )
        gh[...] = dot(mt[...], wh_ref[...]) + bh_ref[...]
        for j in range((own_rows + far_rows) // LANES):
            pmat[:, j * LANES : (j + 1) * LANES] = onehot(place[b] == lane + j * LANES)
        if ready and b + 1 < batches:
            build(b + 1, 0, own_rows + doms * far_rows, 0)

        drain(recv.at[b, pl.ds(cap, own_rows - cap)], OWN_R + b)
        drain(recv.at[b, pl.ds(own_rows + ocap, far_rows - ocap)], FAR_R + b)
        ms = dot(pmat[...], recv[b]).astype(BF)
        msg[...] = (part[...] + dot(ms, wm_ref[width : 2 * width, :])).astype(BF)

        @pl.loop(0, events // 128)
        def _(i):
            at = pl.ds(pl.multiple_of(i * 128, 128), 128)
            avg = (dot(emat[at, :], msg[...]) / cnt[at, :]).astype(BF)
            gi = dot(avg, wi_ref[...]) + bi_ref[...]
            g = gh[at, :]
            reset = jax.nn.sigmoid(gi[:, :width] + g[:, :width])
            update = jax.nn.sigmoid(
                gi[:, width : 2 * width] + g[:, width : 2 * width]
            )
            cand = jnp.tanh(gi[:, 2 * width :] + reset * g[:, 2 * width :])
            prev = mt[at, :].astype(F32)
            fresh[at, :] = ((1.0 - update) * cand + update * prev).astype(BF)

        @pl.loop(0, nodes // 512)
        def _(i):
            at = pl.ds(pl.multiple_of(i * 512, 512), 512)
            new = dot(smat[at, :], fresh[...])
            out_ref[at, :] = jnp.where(
                touched[at, :] > 0.0, new, table[at, :].astype(F32)
            ).astype(BF)

    drain(ids_send.at[pl.ds(8, rows * 8 - 8)], IDS_S)
    if doms > 1:
        drain(ids_recv.at[pl.ds(1, doms - 1)], IDD_S)
    for b in range(batches):
        drain(send.at[b, pl.ds(cap, own_rows - cap)], OWN_S + b)
        drain(fars.at[b, pl.ds(ocap, far_rows - ocap)], FAR_S + b)
        if doms > 1:
            drain(domr.at[b], DOM_S + b)


def shards(
    memory,
    node_time,
    target,
    source,
    event_time,
    edge_feat,
    owner_group,
    w_message,
    frequency,
    phase_shift,
    w_input,
    w_hidden,
    bias_input,
    bias_hidden,
):
    nodes, width = memory.shape
    batches, events = target.shape
    rows = lax.axis_size("row")
    doms = lax.axis_size("dom")
    cap = -(-(3 * events // (2 * rows)) // 16) * 16
    ocap = -(-(events // (2 * rows)) // 16) * 16
    slots = rows * (cap + ocap)
    total = rows * cap + doms * rows * ocap
    ready = total <= 2048
    gates = w_input.shape[1]
    nt = node_time.reshape(nodes // LANES, LANES)
    nt = jnp.stack([nt >> 8, nt & 255]).astype(BF)
    owner = jnp.broadcast_to(owner_group[:, None], (batches, width))
    cfg = (doms, rows, nodes, events, width, batches, cap, ocap, ready)
    vm = pltpu.VMEM
    return pl.pallas_call(
        functools.partial(kernel, cfg),
        out_shape=jax.ShapeDtypeStruct((nodes, width), BF),
        in_specs=[pl.BlockSpec(memory_space=vm)] * 14,
        out_specs=pl.BlockSpec(memory_space=vm),
        scratch_shapes=[
            vm((rows * 8, LANES), I32),
            vm((doms, rows * 8, LANES), I32),
            vm((batches, total, LANES), I32),
            vm((total if ready else max(rows * cap // 2, rows * ocap), nodes), BF),
            vm((batches, total, width), BF),
            vm((batches, slots, width), BF),
            vm((batches, max(doms - 1, 1), rows * ocap, width), BF),
            vm((batches, rows * ocap, width), BF),
            vm((batches, events, 1), I32),
            vm((events, nodes), BF),
            vm((nodes, events), BF),
            vm((nodes, 1), F32),
            vm((events, slots), BF),
            vm((events, events), BF),
            vm((events, 1), F32),
            vm((events, width), BF),
            vm((events, width), F32),
            vm((events, gates), F32),
            vm((events, width), BF),
            vm((events, width), BF),
            pltpu.SemaphoreType.DMA((4 + 6 * batches,)),
        ],
        compiler_params=pltpu.CompilerParams(
            collective_id=0,
            has_side_effects=True,
            vmem_limit_bytes=60 * 1024 * 1024,
        ),
    )(
        memory,
        nt,
        target,
        source,
        event_time,
        edge_feat,
        owner,
        w_message,
        frequency.reshape(1, -1),
        phase_shift.reshape(1, -1),
        w_input,
        w_hidden,
        bias_input.reshape(1, -1),
        bias_hidden.reshape(1, -1),
    )


def solution(mesh):
    in_specs = (
        P(("dom", "row"), None),
        P(("dom", "row")),
        P(None, ("dom", "row")),
        P(None, ("dom", "row")),
        P(None, ("dom", "row")),
        P(None, ("dom", "row"), None),
        P(),
        P(),
        P(),
        P(),
        P(),
        P(),
        P(),
        P(),
    )
    out_specs = P(("dom", "row"), None)
    return jax.shard_map(shards, mesh=mesh, in_specs=in_specs, out_specs=out_specs, check_vma=False)
```

profile of v0, /device:TPU:0, one launch (start us, length us, event | category | flops | bytes accessed | tf_op | source)
XLA Modules:
  0.0 97.3 jit_solution(16828192104810611308)
XLA Ops:
  0.0 0.0 copy-start.1
  0.0 0.0 copy-start
  0.0 1.3 %reshape.42.bi_ref = f32[1,768]{1,0:T(1,128)} reshape(f32[768]{0:T(1024)} %param.26) | data formatting | bytes 6144 | tf_op jit(solution)/shard_map/reshape | solution.py:406
  1.3 0.0 copy-done.1
  1.3 0.0 copy-start.2
  1.3 0.6 reshape.43.bh_ref
  1.9 0.1 copy-done.2
  2.0 0.7 broadcast_in_dim.2.owner_ref
  2.6 0.0 copy-done
  2.6 0.6 pad_maximum_fusion.nt_ref
  3.2 91.8 %shard_map.136 = bf16[2048,256]{1,0:T(8,128)(2,1)} custom-call(bf16[2048,256]{1,0:T(8,128)(2,1)} %mem_ref.1, bf16[2,16,128]{2,1,0:T(8,128)(2,1)} %pad_maximum_fusion.nt_ref, s32[4,512]{1,0:T(4,128)} %tgt_ref.1, s32[4,512]{1,0:T(4,128)} %src_ref.1, s32[4,512]{1,0:T(4,128)} %et_ref.1, bf16[4,512,128]{2,1,0:T(8,128)(2,1)} %edge_ref.1, ...), custom_call_target="tpu_custom_call" | custom-call | tf_op jit(solution)/shard_map/pallas_call | solution.py:360
  95.0 2.3 %copy.16 = bf16[2048,256]{1,0:T(8,128)(2,1)} copy(bf16[2048,256]{1,0:T(8,128)(2,1)} %shard_map.136) | data formatting | bytes 2097152
  (1 shorter events, 0.0 us)
Async XLA Ops:
  0.0 1.3 %copy-start.1 = (f32[768]{0:T(1024)S(1)}, f32[768]{0:T(1024)}, u32[]{:S(2)}) copy-start(f32[768]{0:T(1024)} %param.27) | copy-start | bytes 9220
  0.0 2.6 %copy-start = (s32[2048]{0:T(1024)S(1)}, s32[2048]{0:T(1024)}, u32[]{:S(2)}) copy-start(s32[2048]{0:T(1024)} %param.15) | copy-start | bytes 24580
  1.3 0.7 copy-start.2
where the time goes:
time: 97.5 us; the launch traced here: 97.3 us
  Pallas kernels  91.8 us (94%)
  local copies, waits for them, and re-layouts  4.89 us (5%)
    pallas_call x1, Pallas kernels, shards(): pl.pallas_call(functools.partial(kernel, cfg), out_shape=jax.ShapeDtypeSt...  91.8 us
    unnamed x7, local copies, waits for them, and re-layouts  2.35 us

commit v1 on v0

--- a/solution.py
+++ b/solution.py
@@ -61,8 +61,11 @@
     mt,
     part,
     gh,
-    msg,
+    gi,
     fresh,
+    qmat,
+    hits,
+    turned,
     sems,
 ):
     doms, rows, nodes, events, width, batches, cap, ocap, ready = cfg
@@ -72,6 +75,7 @@
     node_bits = nodes.bit_length() - 1
     own_rows = rows * cap
     far_rows = rows * ocap
+    total = own_rows + doms * far_rows
     IDS_S, IDS_R, IDD_S, IDD_R = range(4)
     OWN_S, OWN_R, DOM_S, DOM_R, FAR_S, FAR_R = (4 + batches * i for i in range(6))
 
@@ -148,27 +152,25 @@
     for q in range(1, doms):
         push(ids_recv.at[0], ids_recv.at[doms - q], IDD_S, IDD_R, dom_peer(q))
 
-    def spread(q):
-        turned = ids_recv[q].astype(F32).T.astype(I32)
-        for b in range(batches):
-            for k in range(rows):
-                col = turned[:, k * 8 + b : k * 8 + b + 1]
-                if q == 0:
-                    colid[b, k * cap : (k + 1) * cap, :] = jnp.broadcast_to(
-                        col[:cap], (cap, LANES)
-                    )
-                at = own_rows + q * far_rows + k * ocap
-                colid[b, at : at + ocap, :] = jnp.broadcast_to(
-                    col[cap : cap + ocap], (ocap, LANES)
+    def spread(q, b):
+        for k in range(rows):
+            col = turned[q, :, k * 8 + b : k * 8 + b + 1]
+            if q == 0:
+                colid[k * cap : (k + 1) * cap, :] = jnp.broadcast_to(
+                    col[:cap], (cap, LANES)
                 )
-
-    def build(b, start, count, to):
-        step = LANES
+            at = own_rows + q * far_rows + k * ocap
+            colid[at : at + ocap, :] = jnp.broadcast_to(
+                col[cap : cap + ocap], (ocap, LANES)
+            )
+
+    def build(start, count, to):
+        step = 64
         lanes = iota((step, LANES), 1)
 
         @pl.loop(0, count // step)
         def _(i):
-            c = colid[b, pl.ds(pl.multiple_of(start + i * step, step), step), :]
+            c = colid[pl.ds(pl.multiple_of(start + i * step, step), step), :]
             for j in range(nodes // LANES):
                 gmat[
                     pl.ds(pl.multiple_of(to + i * step, step), step),
@@ -180,26 +182,80 @@
             at = start
         else:
             at = 0
-            build(b, start, count, 0)
+            build(start, count, 0)
         found = dot(gmat[at : at + count, :], table[...]).astype(BF)
         send[b, start : start + count, :] = found
 
-    spread(0)
+    def link(s_row):
+        step = 64
+
+        @pl.loop(0, total // step)
+        def _(i):
+            at = pl.ds(pl.multiple_of(i * step, step), step)
+            c = colid[at, :]
+            met = jnp.zeros((step, LANES), F32)
+            for j in range(events // LANES):
+                hit = jnp.where(c == s_row[:, j * LANES : (j + 1) * LANES], 1.0, 0.0)
+                qmat[at, j * LANES : (j + 1) * LANES] = hit.astype(BF)
+                met += hit
+            hits[at, :] = jnp.sum(met, axis=1, keepdims=True)
+
+    def renew(b, start, count):
+        at = slice(start, start + count)
+        send[b, at, :] = jnp.where(
+            hits[at, :] > 0.0, dot(qmat[at, :], fresh[...]), send[b, at, :].astype(F32)
+        ).astype(BF)
+
+    def settle(old):
+        @pl.loop(0, nodes // 512)
+        def _(i):
+            at = pl.ds(pl.multiple_of(i * 512, 512), 512)
+            new = dot(smat[at, :], fresh[...])
+            out_ref[at, :] = jnp.where(
+                touched[at, :] > 0.0, new, old[at, :].astype(F32)
+            ).astype(BF)
+
+    def row_of(ref):
+        return jnp.concatenate(
+            [ref[i : i + 1, :] for i in range(ref.shape[0])], axis=1
+        )
+
+    bias_i = row_of(bi_ref)
+    bias_h = row_of(bh_ref)
+    bias_wide = bias_h + jnp.where(
+        iota(bias_i.shape, 1) < 2 * width, bias_i, jnp.zeros_like(bias_i)
+    )
+
+    turned[0] = ids_recv[0].astype(F32).T.astype(I32)
+    spread(0, 0)
     if ready:
-        build(0, 0, own_rows + far_rows, 0)
+        build(0, own_rows + far_rows, 0)
     if doms > 1:
         drain(ids_recv.at[pl.ds(1, doms - 1)], IDD_R)
     for q in range(1, doms):
-        spread(q)
+        turned[q] = ids_recv[q].astype(F32).T.astype(I32)
+        spread(q, 0)
     if ready and doms > 1:
-        build(0, own_rows + far_rows, (doms - 1) * far_rows, own_rows + far_rows)
-
-    half = own_rows // 2
+        build(own_rows + far_rows, (doms - 1) * far_rows, own_rows + far_rows)
+
+    quarter = rows // 4
+    parts = (
+        (quarter, 3 * quarter),
+        (0, quarter),
+        (3 * quarter, rows),
+    )
     for b in range(batches):
         table = mem_ref if b == 0 else out_ref
+
+        def supply(start, count):
+            if b == 0:
+                gather(0, table, start, count)
+            else:
+                renew(b, start, count)
+
         for q in range(1, doms):
             at = own_rows + q * far_rows
-            gather(b, table, at, far_rows)
+            supply(at, far_rows)
             push(
                 send.at[b, pl.ds(at, far_rows)],
                 domr.at[b, doms - q - 1],
@@ -207,11 +263,9 @@
                 DOM_R + b,
                 dom_peer(q),
             )
-        for h in range(2):
-            gather(b, table, h * half, half)
-            if h == 0:
-                recv[b, 0:cap, :] = send[b, 0:cap, :]
-            for k in range(max(1, h * rows // 2), (h + 1) * rows // 2):
+        for first, last in parts:
+            supply(first * cap, (last - first) * cap)
+            for k in sorted(range(max(1, first), last), key=lambda k: abs(2 * k - rows)):
                 push(
                     send.at[b, pl.ds(k * cap, cap)],
                     recv.at[b, pl.ds((rows - k) * cap, cap)],
@@ -219,7 +273,10 @@
                     OWN_R + b,
                     row_peer(k),
                 )
-        gather(b, table, own_rows, far_rows)
+        supply(own_rows, far_rows)
+        recv[b, 0:cap, :] = send[b, 0:cap, :]
+        if b > 0:
+            settle(mem_ref if b == 1 else out_ref)
 
         t_col = cols[:, b : b + 1]
         t_row = tgt_ref[b : b + 1, :]
@@ -228,7 +285,7 @@
             tmat[:, j * LANES : (j + 1) * LANES] = onehot(t_wide == lane + j * LANES)
         mt[...] = dot(tmat[...], table[...]).astype(BF)
 
-        owner = owner_ref[b : b + 1, :]
+        owner = jnp.full((1, width), owner_ref[b], I32)
         if doms > 1:
             drain(domr.at[b], DOM_R + b)
         picked = send[b, own_rows : own_rows + far_rows, :].astype(F32)
@@ -237,7 +294,7 @@
                 owner == lax.rem(me_d + q, doms), domr[b, q - 1].astype(F32), picked
             )
         fars[b] = picked.astype(BF)
-        for k in range(1, rows):
+        for k in sorted(range(1, rows), key=lambda k: abs(2 * k - rows)):
             push(
                 fars.at[b, pl.ds(k * ocap, ocap)],
                 recv.at[b, pl.ds(own_rows + (rows - k) * ocap, ocap)],
@@ -250,11 +307,11 @@
         same = jnp.logical_and(t_col == t_row, t_col >= 0)
         same_f = jnp.where(same, 1.0, 0.0)
         emat[...] = same_f.astype(BF)
-        cnt[...] = jnp.maximum(jnp.sum(same_f, axis=1, keepdims=True), 1.0)
+        cnt[...] = 1.0 / jnp.maximum(jnp.sum(same_f, axis=1, keepdims=True), 1.0)
         before = jnp.sum(
             jnp.where(sub_e < lane_e, same_f, 0.0), axis=0, keepdims=True
         )
-        s_row = jnp.where(before > 0.0, -1, t_row)
+        s_row = jnp.where(jnp.logical_or(before > 0.0, t_row < 0), -2, t_row)
 
         @pl.loop(0, nodes // 256)
         def _(i):
@@ -263,8 +320,9 @@
             smat[pl.ds(at, 256), :] = hit.astype(BF)
             touched[pl.ds(at, 256), :] = jnp.sum(hit, axis=1, keepdims=True)
 
-        hi_part = dot(onehot((t_col >> 7) == iota((events, nodes // LANES), 1)), nt_ref[0])
-        lo_part = dot(onehot((t_col >> 7) == iota((events, nodes // LANES), 1)), nt_ref[1])
+        block = onehot((t_col >> 7) == iota((events, nodes // LANES), 1))
+        hi_part = dot(block, (nt_ref[...] >> 8).astype(F32).astype(BF))
+        lo_part = dot(block, jnp.bitwise_and(nt_ref[...], 255).astype(F32).astype(BF))
         hit = jnp.bitwise_and(t_col, LANES - 1) == lane
         seen = jnp.sum(
             jnp.where(hit, hi_part * 256.0 + lo_part, 0.0), axis=1, keepdims=True
@@ -283,39 +341,43 @@
             + dot(encoded, wm_ref[2 * width : 2 * width + tw, :])
             + dot(edge_ref[b], wm_ref[2 * width + tw :, :])
         )
-        gh[...] = dot(mt[...], wh_ref[...]) + bh_ref[...]
+        gh[...] = dot(mt[...], wh_ref[...]) + bias_wide
         for j in range((own_rows + far_rows) // LANES):
             pmat[:, j * LANES : (j + 1) * LANES] = onehot(place[b] == lane + j * LANES)
-        if ready and b + 1 < batches:
-            build(b + 1, 0, own_rows + doms * far_rows, 0)
+        if b + 1 < batches:
+            for q in range(doms):
+                spread(q, b + 1)
+            if ready:
+                build(0, total, 0)
+            for start, count in (
+                (0, own_rows // 2),
+                (own_rows // 2, own_rows // 2),
+                *((own_rows + q * far_rows, far_rows) for q in range(doms)),
+            ):
+                gather(b + 1, table, start, count)
+            link(s_row)
 
         drain(recv.at[b, pl.ds(cap, own_rows - cap)], OWN_R + b)
+        near = dot(pmat[:, :own_rows], recv[b, :own_rows, :])
         drain(recv.at[b, pl.ds(own_rows + ocap, far_rows - ocap)], FAR_R + b)
-        ms = dot(pmat[...], recv[b]).astype(BF)
-        msg[...] = (part[...] + dot(ms, wm_ref[width : 2 * width, :])).astype(BF)
-
-        @pl.loop(0, events // 128)
-        def _(i):
-            at = pl.ds(pl.multiple_of(i * 128, 128), 128)
-            avg = (dot(emat[at, :], msg[...]) / cnt[at, :]).astype(BF)
-            gi = dot(avg, wi_ref[...]) + bi_ref[...]
+        ms = (near + dot(pmat[:, own_rows:], recv[b, own_rows:, :])).astype(BF)
+        msg = (part[...] + dot(ms, wm_ref[width : 2 * width, :])).astype(BF)
+        avg = (dot(emat[...], msg) * cnt[...]).astype(BF)
+        gi[...] = dot(avg, wi_ref[...])
+
+        for i in range(events // 64):
+            at = slice(i * 64, (i + 1) * 64)
             g = gh[at, :]
-            reset = jax.nn.sigmoid(gi[:, :width] + g[:, :width])
-            update = jax.nn.sigmoid(
-                gi[:, width : 2 * width] + g[:, width : 2 * width]
-            )
-            cand = jnp.tanh(gi[:, 2 * width :] + reset * g[:, 2 * width :])
+            gates = 0.5 * jnp.tanh(0.5 * (gi[at, : 2 * width] + g[:, : 2 * width])) + 0.5
+            reset = gates[:, :width]
+            update = gates[:, width:]
+            cand = jnp.tanh(
+                gi[at, 2 * width :] + bias_i[:, 2 * width :] + reset * g[:, 2 * width :]
+            )
             prev = mt[at, :].astype(F32)
             fresh[at, :] = ((1.0 - update) * cand + update * prev).astype(BF)
 
-        @pl.loop(0, nodes // 512)
-        def _(i):
-            at = pl.ds(pl.multiple_of(i * 512, 512), 512)
-            new = dot(smat[at, :], fresh[...])
-            out_ref[at, :] = jnp.where(
-                touched[at, :] > 0.0, new, table[at, :].astype(F32)
-            ).astype(BF)
-
+    settle(out_ref if batches > 1 else mem_ref)
     drain(ids_send.at[pl.ds(8, rows * 8 - 8)], IDS_S)
     if doms > 1:
         drain(ids_recv.at[pl.ds(1, doms - 1)], IDD_S)
@@ -353,19 +415,19 @@
     ready = total <= 2048
     gates = w_input.shape[1]
     nt = node_time.reshape(nodes // LANES, LANES)
-    nt = jnp.stack([nt >> 8, nt & 255]).astype(BF)
-    owner = jnp.broadcast_to(owner_group[:, None], (batches, width))
     cfg = (doms, rows, nodes, events, width, batches, cap, ocap, ready)
     vm = pltpu.VMEM
     return pl.pallas_call(
         functools.partial(kernel, cfg),
         out_shape=jax.ShapeDtypeStruct((nodes, width), BF),
-        in_specs=[pl.BlockSpec(memory_space=vm)] * 14,
+        in_specs=[
+            pl.BlockSpec(memory_space=pltpu.SMEM if i == 6 else vm) for i in range(14)
+        ],
         out_specs=pl.BlockSpec(memory_space=vm),
         scratch_shapes=[
             vm((rows * 8, LANES), I32),
             vm((doms, rows * 8, LANES), I32),
-            vm((batches, total, LANES), I32),
+            vm((total, LANES), I32),
             vm((total if ready else max(rows * cap // 2, rows * ocap), nodes), BF),
             vm((batches, total, width), BF),
             vm((batches, slots, width), BF),
@@ -381,8 +443,11 @@
             vm((events, width), BF),
             vm((events, width), F32),
             vm((events, gates), F32),
+            vm((events, gates), F32),
             vm((events, width), BF),
-            vm((events, width), BF),
+            vm((total, events), BF),
+            vm((total, 1), F32),
+            vm((doms, LANES, rows * 8), I32),
             pltpu.SemaphoreType.DMA((4 + 6 * batches,)),
         ],
         compiler_params=pltpu.CompilerParams(
@@ -397,14 +462,14 @@
         source,
         event_time,
         edge_feat,
-        owner,
+        owner_group,
         w_message,
         frequency.reshape(1, -1),
         phase_shift.reshape(1, -1),
         w_input,
         w_hidden,
-        bias_input.reshape(1, -1),
-        bias_hidden.reshape(1, -1),
+        bias_input.reshape(-1, LANES),
+        bias_hidden.reshape(-1, LANES),
     )
 
 

time: 97.5 us -> 82.4 us (0.85)
  Pallas kernels: 91.8 us -> 80 us
  local copies, waits for them, and re-layouts: 4.89 us -> 2.26 us
    pallas_call x1, Pallas kernels: 91.8 us -> 80 us  [shards(): pl.pallas_call(functools.partial(kernel, cfg), out_shape=jax.ShapeDtypeSt...]
    reshape x2 -> x0, local copies, waits for them, and re-layouts: 1.89 us -> none  [the longest x1 1.31 us: shards(): bias_input.reshape(1, -1)]
    unnamed x7 -> x1, local copies, waits for them, and re-layouts: 2.35 us -> 2.26 us
where the time goes in v1:
time: 82.4 us; the launch traced here: 82.3 us
  Pallas kernels  80 us (97%)
  local copies, waits for them, and re-layouts  2.26 us (3%)
    pallas_call x1, Pallas kernels, shards(): pl.pallas_call(functools.partial(kernel, cfg), out_shape=jax.ShapeDtypeSt...  80 us
    unnamed x1, local copies, waits for them, and re-layouts  2.26 us

profile of v1, /device:TPU:0, one launch (start us, length us, event | category | flops | bytes accessed | tf_op | source)
XLA Modules:
  0.0 82.3 jit_solution(155748297884299995)
XLA Ops:
  0.0 80.0 %shard_map.136 = bf16[2048,256]{1,0:T(8,128)(2,1)} custom-call(bf16[2048,256]{1,0:T(8,128)(2,1)} %mem_ref.1, s32[16,128]{1,0:T(8,128)} %bitcast.5, s32[4,512]{1,0:T(4,128)} %tgt_ref.1, s32[4,512]{1,0:T(4,128)} %src_ref.1, s32[4,512]{1,0:T(4,128)} %et_ref.1, bf16[4,512,128]{2,1,0:T(8,128)(2,1)} %edge_ref.1, s32[4]{0:T(128)} %owner_ref.1, ...), custom_call_target="tpu_custom_call" | custom-call | tf_op jit(solution)/shard_map/pallas_call | solution.py:420
  80.0 2.3 %copy.16 = bf16[2048,256]{1,0:T(8,128)(2,1)} copy(bf16[2048,256]{1,0:T(8,128)(2,1)} %shard_map.136) | data formatting | bytes 2097152

commit v2 on v1

--- a/solution.py
+++ b/solution.py
@@ -229,14 +229,16 @@
     turned[0] = ids_recv[0].astype(F32).T.astype(I32)
     spread(0, 0)
     if ready:
-        build(0, own_rows + far_rows, 0)
-    if doms > 1:
-        drain(ids_recv.at[pl.ds(1, doms - 1)], IDD_R)
-    for q in range(1, doms):
-        turned[q] = ids_recv[q].astype(F32).T.astype(I32)
-        spread(q, 0)
-    if ready and doms > 1:
-        build(own_rows + far_rows, (doms - 1) * far_rows, own_rows + far_rows)
+        build(0, own_rows, 0)
+
+    def rest_of_ids():
+        if doms > 1:
+            drain(ids_recv.at[pl.ds(1, doms - 1)], IDD_R)
+        for q in range(1, doms):
+            turned[q] = ids_recv[q].astype(F32).T.astype(I32)
+            spread(q, 0)
+        if ready:
+            build(own_rows, doms * far_rows, own_rows)
 
     quarter = rows // 4
     parts = (
@@ -253,26 +255,37 @@
             else:
                 renew(b, start, count)
 
-        for q in range(1, doms):
-            at = own_rows + q * far_rows
-            supply(at, far_rows)
-            push(
-                send.at[b, pl.ds(at, far_rows)],
-                domr.at[b, doms - q - 1],
-                DOM_S + b,
-                DOM_R + b,
-                dom_peer(q),
-            )
-        for first, last in parts:
-            supply(first * cap, (last - first) * cap)
-            for k in sorted(range(max(1, first), last), key=lambda k: abs(2 * k - rows)):
+        def send_dom():
+            for q in range(1, doms):
+                at = own_rows + q * far_rows
+                supply(at, far_rows)
                 push(
-                    send.at[b, pl.ds(k * cap, cap)],
-                    recv.at[b, pl.ds((rows - k) * cap, cap)],
-                    OWN_S + b,
-                    OWN_R + b,
-                    row_peer(k),
+                    send.at[b, pl.ds(at, far_rows)],
+                    domr.at[b, doms - q - 1],
+                    DOM_S + b,
+                    DOM_R + b,
+                    dom_peer(q),
                 )
+
+        def send_own():
+            for first, last in parts:
+                supply(first * cap, (last - first) * cap)
+                for k in sorted(range(max(1, first), last), key=lambda k: abs(2 * k - rows)):
+                    push(
+                        send.at[b, pl.ds(k * cap, cap)],
+                        recv.at[b, pl.ds((rows - k) * cap, cap)],
+                        OWN_S + b,
+                        OWN_R + b,
+                        row_peer(k),
+                    )
+
+        if b == 0:
+            send_own()
+            rest_of_ids()
+            send_dom()
+        else:
+            send_dom()
+            send_own()
         supply(own_rows, far_rows)
         recv[b, 0:cap, :] = send[b, 0:cap, :]
         if b > 0:

time: 82.4 us -> 82.3 us (level)
  no operation moved by 1% of the time
where the time goes in v2:
time: 82.3 us; the launch traced here: 82.1 us
  Pallas kernels  79.8 us (97%)
  local copies, waits for them, and re-layouts  2.26 us (3%)
    pallas_call x1, Pallas kernels, shards(): pl.pallas_call(functools.partial(kernel, cfg), out_shape=jax.ShapeDtypeSt...  79.8 us
    unnamed x1, local copies, waits for them, and re-layouts  2.26 us

profile of v2, /device:TPU:0, one launch (start us, length us, event | category | flops | bytes accessed | tf_op | source)
XLA Modules:
  0.0 82.1 jit_solution(12517770582135375240)
XLA Ops:
  0.0 79.8 %shard_map.136 = bf16[2048,256]{1,0:T(8,128)(2,1)} custom-call(bf16[2048,256]{1,0:T(8,128)(2,1)} %mem_ref.1, s32[16,128]{1,0:T(8,128)} %bitcast.5, s32[4,512]{1,0:T(4,128)} %tgt_ref.1, s32[4,512]{1,0:T(4,128)} %src_ref.1, s32[4,512]{1,0:T(4,128)} %et_ref.1, bf16[4,512,128]{2,1,0:T(8,128)(2,1)} %edge_ref.1, s32[4]{0:T(128)} %owner_ref.1, ...), custom_call_target="tpu_custom_call" | custom-call | tf_op jit(solution)/shard_map/pallas_call | solution.py:433
  79.8 2.3 %copy.16 = bf16[2048,256]{1,0:T(8,128)(2,1)} copy(bf16[2048,256]{1,0:T(8,128)(2,1)} %shard_map.136) | data formatting | bytes 2097152
